TPU v7x, 32 devices: a whole 2x2x4 slice. The times are simulated.
32 devices in a mesh: blk: 16 (over z, x, core), win: 2 (over y).
Axes of the slice: x: 2, y: 2, z: 4, core: 2. Of those that a mesh axis runs over, the one named last changes fastest.
Arguments:
- traces: bfloat16 [8, 512, 8192], P('win', None, 'blk'), may hold values from -256 to 256, as said below
- channel_mask: int32 [8192], P('blk'), may hold values 0 or 1
Outputs:
- cross: float32 [4, 2, 2, 8192, 512], P(None, 'win', None, 'blk')
Inputs may be any that keep to these rules, and one draw needn't show every extreme that they name: traces are noise records of the channels with different amplitudes.
All inputs are finite; a program needn't handle non-finite values. No bound on the sum of `channel_mask` on one device may be relied on, other than what follows from the above.
Results may differ from a plain program's by a relative error of at most 0.0049.
Values may be sent and summed in bfloat16 or wider, within the bound.
A program may use at most 64 MiB of HBM per device.

v0:
```python
import math

import jax
import jax.numpy as jnp
from jax import lax
from jax.sharding import PartitionSpec as P

ROUNDS = 4


water_level = 0.5


def shifted(value, axis, steps):
    count = lax.axis_size(axis)
    pairs = [(source, (source + steps) % count) for source in range(count)]
    return lax.ppermute(value, axis, pairs)


def dft_table(samples_len, band_count):
    row_index = jnp.arange(samples_len, dtype=jnp.int32)
    per_band = samples_len // band_count
    half_rows = per_band // 2
    freq_bin = row_index // per_band * half_rows + row_index % per_band % half_rows
    imag_rows = row_index % per_band >= half_rows
    time_index = jnp.arange(samples_len, dtype=jnp.int32)
    phase_int = freq_bin[:, None] * time_index[None, :] % samples_len
    angles = 2.0 * math.pi / samples_len * phase_int.astype(jnp.float32)
    hann_taper = 0.5 - 0.5 * jnp.cos(2.0 * math.pi / samples_len * time_index.astype(jnp.float32))
    entries = jnp.where(imag_rows[:, None], -jnp.sin(angles), jnp.cos(angles)) * hann_taper[None, :]
    return entries.astype(jnp.bfloat16)


def regroup(spectra):
    return lax.all_to_all(spectra, "win", split_axis=1, concat_axis=0, tiled=True)


def cross_block(own_block, partner, band_width, norm_scale):
    swapped = jnp.concatenate([partner[:, band_width:], -partner[:, :band_width]], axis=1)
    real_part = jnp.einsum("wqc,wqd->cd", own_block, partner, preferred_element_type=jnp.float32)
    imag_part = jnp.einsum("wqc,wqd->cd", own_block, swapped, preferred_element_type=jnp.float32)
    return jnp.stack([real_part, imag_part]) * norm_scale


def local(traces, channel_mask):
    win_count = lax.axis_size("win")
    local_windows = traces.shape[0]
    samples_len = traces.shape[1]
    windows_all = local_windows * win_count
    bin_count = samples_len // 2
    band_width = bin_count // win_count
    transform = dft_table(samples_len, win_count)
    spectra = jnp.einsum(
        "rt,wtc->wrc", transform, traces, preferred_element_type=jnp.float32
    ).astype(jnp.bfloat16)
    mask_float = channel_mask.astype(jnp.float32)
    regrouped = regroup(spectra)
    spec_f32 = regrouped.astype(jnp.float32)
    power_mean = (
        jnp.sum(spec_f32[:, :band_width] ** 2 + spec_f32[:, band_width:] ** 2, axis=0) / windows_all
    )
    level_mean = lax.psum(jnp.sum(power_mean, axis=0), "win") / bin_count
    factor = mask_float[None, :] / jnp.sqrt(power_mean + water_level * level_mean[None, :] + 1e-06)
    doubled = jnp.concatenate([factor, factor], axis=0)
    white = (spec_f32 * doubled[None]).astype(jnp.bfloat16)
    norm_scale = 1.0 / math.sqrt(windows_all * band_width)
    results = []
    current = white
    for offset in range(ROUNDS):
        current = shifted(current, "blk", -1)
        results.append(cross_block(white, current, band_width, norm_scale))
    return jnp.stack(results)[:, None]


def solution(mesh):
    return jax.shard_map(
        local,
        mesh=mesh,
        in_specs=(P("win", None, "blk"), P("blk")),
        out_specs=P(None, "win", None, "blk", None),
        check_vma=False,
    )
```

profile of v0, /device:TPU:27, one launch (start us, length us, event | category | flops | bytes accessed | tf_op | source)
XLA Modules:
  0.0 170.4 jit_solution(8644152144192286727)
XLA Ops:
  0.0 0.0 copy-start
  0.1 1.5 copy-done
  1.6 6.1 %convert_bitcast_fusion = bf16[4,512,512]{2,1,0:T(8,128)(2,1)S(1)} fusion(bf16[4,512,512]{2,1,0:T(8,128)(2,1)S(1)} %copy-done, f32[512]{0:T(512)S(1)} %multiply_subtract_fusion, s32[512]{0:T(512)S(1)} %fusion.47, pred[512]{0:T(512)(128)(4,1)S(1)} %fusion.51), kind=kOutput, calls=%fused_computation.26 | convolution fusion | flops 1079508992 | bytes 4198912 | tf_op jit(solution)/shard_map/rt,wtc->wrc/dot_general | solution.py:53
  7.7 2.9 %copy.13 = bf16[4,512,512]{2,0,1:T(4,128)(2,1)} copy(bf16[4,512,512]{2,1,0:T(8,128)(2,1)S(1)} %convert_bitcast_fusion) | data formatting | bytes 4194304 | tf_op jit(solution)/shard_map/convert_element_type | solution.py:55
  10.6 0.0 copy-start.2
  10.6 4.9 %all-to-all-start = ((bf16[4,512,512]{2,0,1:T(4,128)(2,1)}), bf16[4,512,512]{2,0,1:T(4,128)(2,1)}, u32[]{:S(2)}, u32[]{:S(2)}) async-start(bf16[4,512,512]{2,0,1:T(4,128)(2,1)} %copy.13), calls=%async_computation | async-start | bytes 4194304 | tf_op jit(solution)/shard_map/all_to_all | solution.py:35
  15.5 0.0 copy-done.2
  15.6 24.3 %all-to-all-done = bf16[4,512,512]{2,0,1:T(4,128)(2,1)} async-done(((bf16[4,512,512]{2,0,1:T(4,128)(2,1)}), bf16[4,512,512]{2,0,1:T(4,128)(2,1)}, u32[]{:S(2)}, u32[]{:S(2)}) %all-to-all-start) | async-done | bytes 2097184 | tf_op jit(solution)/shard_map/all_to_all | solution.py:35
  39.9 2.2 %copy.14 = f32[4,2,256,512]{3,2,0,1:T(8,128)S(1)} copy(bf16[4,2,256,512]{3,0,2,1:T(4,128)(2,1)} %bitcast.24) | data formatting | bytes 6291456 | tf_op jit(solution)/shard_map/convert_element_type | solution.py:58
  42.1 0.0 copy-start.1
  42.1 0.5 fusion.1
  42.7 1.5 copy-done.1
  44.2 3.8 %psum.7 = f32[512]{0:T(512)S(1)} all-reduce(f32[512]{0:T(512)S(1)} %multiply_reduce_fusion), channel_id=1, replica_groups=mesh['blk'=16,'win'=2] {'win'}, use_global_device_ids=true, to_apply=%region_2.3 | all-reduce | flops 512 | bytes 4096 | tf_op jit(solution)/shard_map/psum | solution.py:62
  48.0 0.1 rsqrt_multiply_fusion
  48.0 0.1 pad_maximum_fusion
  48.1 2.8 %multiply_convert_fusion = bf16[8,256,512]{2,1,0:T(8,128)(2,1)S(1)} fusion(f32[256,512]{1,0:T(8,128)S(1)} %pad_maximum_fusion, f32[4,2,256,512]{3,2,0,1:T(8,128)} %copy-done.1), kind=kLoop, calls=%fused_computation.1 | loop fusion | flops 2097152 | bytes 6815744 | tf_op jit(solution)/shard_map/convert_element_type | solution.py:65
  50.9 2.7 %collective-permute-start = (bf16[8,256,512]{2,1,0:T(8,128)(2,1)S(1)}, bf16[8,256,512]{2,1,0:T(8,128)(2,1)S(1)}, u32[]{:S(2)}, u32[]{:S(2)}) collective-permute-start(bf16[8,256,512]{2,1,0:T(8,128)(2,1)S(1)} %multiply_convert_fusion), channel_id=1, source_target_pairs={{0,30},{2,0},{4,2},{6,4},{8,6},{10,8},{12,10},{14,12},{16,14},{18,... | collective-permute-start | bytes 6291464 | tf_op jit(solution)/shard_map/ppermute | solution.py:17
  53.7 25.5 %collective-permute-done = bf16[8,256,512]{2,1,0:T(8,128)(2,1)S(1)} collective-permute-done((bf16[8,256,512]{2,1,0:T(8,128)(2,1)S(1)}, bf16[8,256,512]{2,1,0:T(8,128)(2,1)S(1)}, u32[]{:S(2)}, u32[]{:S(2)}) %collective-permute-start) | collective-permute-done | bytes 2097184 | tf_op jit(solution)/shard_map/ppermute | solution.py:17
  79.1 0.0 collective-permute-start.1
  79.1 28.2 %collective-permute-done.1 = bf16[8,256,512]{2,1,0:T(8,128)(2,1)S(1)} collective-permute-done((bf16[8,256,512]{2,1,0:T(8,128)(2,1)S(1)}, bf16[8,256,512]{2,1,0:T(8,128)(2,1)S(1)}, u32[]{:S(2)}, u32[]{:S(2)}) %collective-permute-start.1) | collective-permute-done | bytes 2097184 | tf_op jit(solution)/shard_map/ppermute | solution.py:17
  107.3 0.0 collective-permute-start.2
  107.3 0.1 fusion.62
  107.4 1.3 fusion.27
  108.7 1.3 convolution_bitcast_fusion.3
  110.0 0.2 maximum_multiply_fusion
  110.2 0.1 fusion.63
  110.4 25.1 %collective-permute-done.2 = bf16[8,256,512]{2,1,0:T(8,128)(2,1)S(1)} collective-permute-done((bf16[8,256,512]{2,1,0:T(8,128)(2,1)S(1)}, bf16[8,256,512]{2,1,0:T(8,128)(2,1)S(1)}, u32[]{:S(2)}, u32[]{:S(2)}) %collective-permute-start.2) | collective-permute-done | bytes 2097184 | tf_op jit(solution)/shard_map/ppermute | solution.py:17
  135.5 0.0 collective-permute-start.3
  135.5 1.3 fusion.24
  136.7 1.3 convolution_bitcast_fusion.2
  138.0 0.2 maximum_multiply_fusion.1
  138.2 0.1 fusion.64
  138.4 1.3 fusion.21
  139.7 1.3 convolution_bitcast_fusion.1
  140.9 0.2 maximum_multiply_fusion.2
  141.2 22.4 %collective-permute-done.3 = bf16[8,256,512]{2,1,0:T(8,128)(2,1)S(1)} collective-permute-done((bf16[8,256,512]{2,1,0:T(8,128)(2,1)S(1)}, bf16[8,256,512]{2,1,0:T(8,128)(2,1)S(1)}, u32[]{:S(2)}, u32[]{:S(2)}) %collective-permute-start.3) | collective-permute-done | bytes 2097184 | tf_op jit(solution)/shard_map/ppermute | solution.py:17
  163.6 0.1 fusion.65
  163.7 1.3 fusion.18
  165.0 1.3 convolution_bitcast_fusion
  166.3 0.2 maximum_multiply_fusion.3
  166.5 3.9 %maximum_bitcast_fusion = f32[4,1,2,512,512]{4,3,2,1,0:T(8,128)} fusion(f32[1,2,512,512]{3,2,1,0:T(8,128)S(1)} %maximum_multiply_fusion.3, f32[1,2,512,512]{3,2,1,0:T(8,128)S(1)} %maximum_multiply_fusion.2, f32[1,2,512,512]{3,2,1,0:T(8,128)S(1)} %maximum_multiply_fusion.1, f32[1,2,512,512]{3,2,1,0:T(8,128)S(1)} %maximum_multiply_fusion), kind=kLoop, calls=%fused_computation | loop fusion | flops 6291456 | bytes 16777216 | tf_op jit(solution)/shard_map/broadcast_in_dim | solution.py:72
  (6 shorter events, 0.1 us)
Async XLA Ops:
  0.0 1.6 copy-start
  10.6 4.9 %copy-start.2 = (s32[512]{0:T(512)S(1)}, s32[512]{0:T(512)}, u32[]{:S(2)}) copy-start(s32[512]{0:T(512)} %param.3) | copy-start | bytes 6148
  10.6 29.3 %all-to-all-start = ((bf16[4,512,512]{2,0,1:T(4,128)(2,1)}), bf16[4,512,512]{2,0,1:T(4,128)(2,1)}, u32[]{:S(2)}, u32[]{:S(2)}) async-start(bf16[4,512,512]{2,0,1:T(4,128)(2,1)} %copy.13), calls=%async_computation | async-start | bytes 4194304 | tf_op jit(solution)/shard_map/all_to_all | solution.py:35
  42.1 2.0 %copy-start.1 = (f32[4,2,256,512]{3,2,0,1:T(8,128)}, f32[4,2,256,512]{3,2,0,1:T(8,128)S(1)}, u32[]{:S(2)}) copy-start(f32[4,2,256,512]{3,2,0,1:T(8,128)S(1)} %copy.14) | copy-start | bytes 12582916
  50.9 28.2 %collective-permute-start = (bf16[8,256,512]{2,1,0:T(8,128)(2,1)S(1)}, bf16[8,256,512]{2,1,0:T(8,128)(2,1)S(1)}, u32[]{:S(2)}, u32[]{:S(2)}) collective-permute-start(bf16[8,256,512]{2,1,0:T(8,128)(2,1)S(1)} %multiply_convert_fusion), channel_id=1, source_target_pairs={{0,30},{2,0},{4,2},{6,4},{8,6},{10,8},{12,10},{14,12},{16,14},{18,... | collective-permute-start | bytes 6291464 | tf_op jit(solution)/shard_map/ppermute | solution.py:17
  79.1 28.2 %collective-permute-start.1 = (bf16[8,256,512]{2,1,0:T(8,128)(2,1)S(1)}, bf16[8,256,512]{2,1,0:T(8,128)(2,1)S(1)}, u32[]{:S(2)}, u32[]{:S(2)}) collective-permute-start(bf16[8,256,512]{2,1,0:T(8,128)(2,1)S(1)} %collective-permute-done), channel_id=1, source_target_pairs={{0,30},{2,0},{4,2},{6,4},{8,6},{10,8},{12,10},{14,12},{16,14},{18,... | collective-permute-start | bytes 6291464 | tf_op jit(solution)/shard_map/ppermute | solution.py:17
  107.3 28.2 %collective-permute-start.2 = (bf16[8,256,512]{2,1,0:T(8,128)(2,1)S(1)}, bf16[8,256,512]{2,1,0:T(8,128)(2,1)S(1)}, u32[]{:S(2)}, u32[]{:S(2)}) collective-permute-start(bf16[8,256,512]{2,1,0:T(8,128)(2,1)S(1)} %collective-permute-done.1), channel_id=1, source_target_pairs={{0,30},{2,0},{4,2},{6,4},{8,6},{10,8},{12,10},{14,12},{16,14},{18,... | collective-permute-start | bytes 6291464 | tf_op jit(solution)/shard_map/ppermute | solution.py:17
  135.5 28.2 %collective-permute-start.3 = (bf16[8,256,512]{2,1,0:T(8,128)(2,1)S(1)}, bf16[8,256,512]{2,1,0:T(8,128)(2,1)S(1)}, u32[]{:S(2)}, u32[]{:S(2)}) collective-permute-start(bf16[8,256,512]{2,1,0:T(8,128)(2,1)S(1)} %collective-permute-done.2), channel_id=1, source_target_pairs={{0,30},{2,0},{4,2},{6,4},{8,6},{10,8},{12,10},{14,12},{16,14},{18,... | collective-permute-start | bytes 6291464 | tf_op jit(solution)/shard_map/ppermute | solution.py:17
where the time goes:
time: 172 us; the launch traced here: 170 us
  waiting for transfers between devices  125 us (73%)
  matrix products  16.2 us (9%)
  other arithmetic  8.93 us (5%)
  local copies, waits for them, and re-layouts  8.17 us (5%)
  starting transfers between devices  7.69 us (4%)
  blocking collectives  3.79 us (2%)
    ppermute x4, waiting for transfers between devices, shifted(): return lax.ppermute(value, axis, pairs)  101 us
    all_to_all x1, waiting for transfers between devices, regroup(): lax.all_to_all(spectra, 'win', split_axis=1, concat_axis=0, tiled=True)  24.3 us
    dot_general x1, matrix products, local(): jnp.einsum('rt,wtc->wrc', transform, traces, preferred_element_type=jnp.f...  6.06 us
    dot_general x4, matrix products, cross_block(): jnp.einsum('wqc,wqd->cd', own_block, partner, preferred_element_type=jnp....  5.07 us
    dot_general x4, matrix products, cross_block(): jnp.einsum('wqc,wqd->cd', own_block, swapped, preferred_element_type=jnp....  5.07 us
    all_to_all x1, starting transfers between devices, regroup(): lax.all_to_all(spectra, 'win', split_axis=1, concat_axis=0, tiled=True)  4.93 us
    broadcast_in_dim x1, other arithmetic, local(): return jnp.stack(results)[:, None]  3.86 us
    psum x1, blocking collectives, local(): level_mean = lax.psum(jnp.sum(power_mean, axis=0), 'win') / bin_count  3.79 us
  transfers between devices with their start and end apart: 5, of which 5 were waited for; matrix products, arithmetic and copies ran while one was open for 5% of the time, Pallas kernels for 0%

commit v1 on v0

v1 whole, which is shorter than its diff:
```python
import functools
import math

import jax
import jax.numpy as jnp
import ml_dtypes
import numpy as np
from jax import lax
from jax.experimental import pallas as pl
from jax.experimental.pallas import tpu as pltpu
from jax.sharding import PartitionSpec as P

ROUNDS = 4
CHUNK_BINS = 16
WATER_LEVEL = 0.5
MESH = pl.DeviceIdType.MESH


def dft_table(samples, bands, bins):
    width = samples // 2 // bands
    order = np.arange(samples // 2).reshape(bands, width // bins, 1, bins)
    order = np.broadcast_to(order, (bands, width // bins, 2, bins))
    time = np.arange(samples)
    phase = order[..., None] * time % samples
    angles = 2.0 * np.pi / samples * phase
    taper = 0.5 - 0.5 * np.cos(2.0 * np.pi / samples * time)
    imag = np.array([False, True])[None, None, :, None, None]
    entries = np.where(imag, -np.sin(angles), np.cos(angles)) * taper
    return entries.reshape(bands, 2 * width, samples).astype(np.float32).astype(ml_dtypes.bfloat16)


def kernel(
    blocks, bands, traces, table, mask, acc,
    buf, stage, gathered, level,
    send_y, recv_y, send_z, send_x, send_sib, recv_blk,
    send_lw, recv_lw, send_lb, recv_lb,
):
    me = lax.axis_index("blk")
    band = lax.axis_index("win")
    core = lax.rem(me, 2)
    odd = lax.rem(me // 2, 2)
    local_windows = traces.shape[0]
    chunks, windows, rows, channels = buf.shape[1:]
    bins = rows // 2
    bin_count = chunks * bins * bands

    def at(step):
        return (lax.rem(me + step + blocks, blocks), band)

    def peer(step):
        return (me, lax.rem(band + step, bands))

    sibling = (me + 1 - 2 * core, band)
    others = [at(s) for s in range(-ROUNDS, ROUNDS + 1) if s] + [peer(d) for d in range(1, bands)]
    barrier = pltpu.get_barrier_semaphore()
    for other in others:
        pl.semaphore_signal(barrier, inc=1, device_id=other, device_id_type=MESH)

    def remote(src, dst, send, recv, target):
        return pltpu.make_async_remote_copy(
            src_ref=src, dst_ref=dst, send_sem=send, recv_sem=recv,
            device_id=target, device_id_type=MESH,
        )

    def copy_y(d, q):
        first = (bands - d) * local_windows
        return remote(
            stage.at[d - 1, q], buf.at[0, q, pl.ds(first, local_windows)],
            send_y.at[d - 1, q], recv_y.at[d - 1, q], peer(d),
        )

    def copy_z(q):
        return remote(buf.at[0, q], buf.at[4, q], send_z.at[q], recv_blk.at[3, q], at(-4))

    def copy_x(slot, step, q):
        return remote(buf.at[slot, q], buf.at[2, q], send_x.at[q], recv_blk.at[1, q], at(step))

    def copy_sib(slot, pair, q):
        return remote(
            buf.at[slot, q], buf.at[1 + 2 * pair, q],
            send_sib.at[pair, q], recv_blk.at[2 * pair, q], sibling,
        )

    def spectrum(which, window):
        rows_of = jnp.dot(table[which], traces[window], preferred_element_type=jnp.float32)
        return rows_of.astype(jnp.bfloat16).reshape(chunks, rows, channels)

    def power(spec):
        total = None
        for w in range(windows):
            re, im = spec(w)
            term = re * re + im * im
            total = term if total is None else total + term
        return total * (1.0 / windows)

    def parts(slot, q):
        def get(w):
            value = buf[slot, q, w].astype(jnp.float32)
            return value[:bins], value[bins:]
        return get

    def own(q):
        for d in range(1, bands):
            copy_y(d, q).wait_recv()
        copy_z(q).start()

        @pl.when(odd == 1)
        def _():
            copy_x(0, -2, q).start()

        @pl.when(core == 1)
        def _():
            copy_sib(0, 0, q).start()

        gathered[0] += power(parts(0, q)).reshape(bins // 8, 8, channels).sum(axis=0)

    def relay(q):
        copy_z(q).wait_recv()

        @pl.when(odd == 0)
        def _():
            copy_x(4, 2, q).start()

        @pl.when(core == 0)
        def _():
            copy_sib(4, 1, q).start()

    def forward(q):
        copy_x(0, -2, q).wait_recv()
        copy_sib(2, core, q).start()

    def factor(slot, spec):
        mean = jnp.sum(level[slot, 0], axis=0, keepdims=True) * (1.0 / bin_count)
        return level[slot, 1][:1] * lax.rsqrt(power(spec) + WATER_LEVEL * mean + 1e-06)

    def cross(q, first):
        spec = parts(0, q)
        scale = factor(0, spec)
        lhs = []
        for w in range(windows):
            re, im = spec(w)
            re, im = re * scale, im * scale
            lhs.append(jnp.concatenate([
                jnp.concatenate([re, -im], axis=1), jnp.concatenate([im, re], axis=1)
            ], axis=0).astype(jnp.bfloat16))
        lhs = jnp.concatenate(lhs, axis=0).T
        for slot in (2, 4, 1, 3):
            if slot in (1, 3):
                copy_sib(0, slot // 2, q).wait_recv()
            spec = parts(slot, q)
            scale = factor(slot, spec)
            rhs = []
            for w in range(windows):
                re, im = spec(w)
                rhs.append(jnp.concatenate([re * scale, im * scale], axis=0).astype(jnp.bfloat16))
            acc[slot - 1] += jnp.dot(
                lhs, jnp.concatenate(rhs, axis=0), preferred_element_type=jnp.float32
            )

    for d in range(1, bands):
        which = lax.rem(band + d, bands)
        for w in range(local_windows):
            stage[d - 1, :, w] = spectrum(which, w)
    pl.semaphore_wait(barrier, len(others))
    for q in range(chunks):
        for d in range(1, bands):
            copy_y(d, q).start()
    for w in range(local_windows):
        buf[0, :, w] = spectrum(band, w)
    gathered[0] = jnp.zeros(gathered.shape[1:], jnp.float32)

    early = (chunks - 1) // 2
    for q in range(chunks):
        own(q)
        if q >= 2 and q % 2 == 0:
            relay(q // 2 - 1)
            if q >= 4:
                forward(q // 2 - 2)

    def copy_lw(d):
        return remote(
            gathered.at[0], gathered.at[bands - d], send_lw.at[d - 1], recv_lw.at[d - 1], peer(d)
        )

    def copy_lb(r):
        return remote(level.at[0], level.at[r], send_lb.at[r - 1], recv_lb.at[r - 1], at(-r))

    for d in range(1, bands):
        copy_lw(d).start()
    level[0, 1] = jnp.broadcast_to(mask[...].astype(jnp.float32), (8, channels))
    for slot in range(ROUNDS):
        acc[slot] = jnp.zeros(acc.shape[1:], jnp.float32)
    for d in range(1, bands):
        copy_lw(d).wait()
    level[0, 0] = jnp.sum(gathered[...], axis=0)
    for r in range(1, ROUNDS + 1):
        copy_lb(r).start()
    for r in range(1, ROUNDS + 1):
        copy_lb(r).wait()

    def late(t, _):
        @pl.when(t < chunks)
        def _():
            relay(t)

        @pl.when((t >= 1) & (t <= chunks))
        def _():
            forward(t - 1)

        @pl.when(t >= 2)
        def _():
            cross(t - 2, False)
        return 0

    if early > 2:
        def catch_up(q, _):
            cross(q, False)
            return 0
        lax.fori_loop(0, early - 2, catch_up, 0)
    lax.fori_loop(early, chunks + 2, late, 0)

    for q in range(chunks):
        for d in range(1, bands):
            copy_y(d, q).wait_send()
        copy_z(q).wait_send()
        copy_x(0, -2, q).wait_send()
        copy_sib(0, 0, q).wait_send()
        copy_sib(0, 1, q).wait_send()


def local(blocks, bands, traces, channel_mask):
    local_windows, samples, channels = traces.shape
    windows = local_windows * bands
    width = samples // 2 // bands
    bins = min(CHUNK_BINS, width)
    chunks = width // bins
    table = jnp.asarray(dft_table(samples, bands, bins))
    vmem = pl.BlockSpec(memory_space=pltpu.VMEM)
    dma = pltpu.SemaphoreType.DMA
    flops = 2 * samples * samples * channels * local_windows
    flops += 2 * ROUNDS * 2 * channels * channels * windows * 2 * width
    acc = pl.pallas_call(
        functools.partial(kernel, blocks, bands),
        out_shape=jax.ShapeDtypeStruct((ROUNDS, 2 * channels, channels), jnp.float32),
        in_specs=[vmem] * 3,
        out_specs=vmem,
        scratch_shapes=[
            pltpu.VMEM((ROUNDS + 1, chunks, windows, 2 * bins, channels), jnp.bfloat16),
            pltpu.VMEM((bands - 1, chunks, local_windows, 2 * bins, channels), jnp.bfloat16),
            pltpu.VMEM((bands, 8, channels), jnp.float32),
            pltpu.VMEM((ROUNDS + 1, 2, 8, channels), jnp.float32),
            dma((bands - 1, chunks)), dma((bands - 1, chunks)),
            dma((chunks,)), dma((chunks,)), dma((2, chunks)), dma((ROUNDS, chunks)),
            dma((bands - 1,)), dma((bands - 1,)), dma((ROUNDS,)), dma((ROUNDS,)),
        ],
        compiler_params=pltpu.CompilerParams(
            collective_id=0, has_side_effects=True, vmem_limit_bytes=48 * 2**20
        ),
        cost_estimate=pl.CostEstimate(flops=flops, bytes_accessed=2**24, transcendentals=0),
    )(traces, table, channel_mask[None])
    norm_scale = 1.0 / math.sqrt(windows * width)
    return (acc * norm_scale).reshape(ROUNDS, 1, 2, channels, channels)


def solution(mesh):
    return jax.shard_map(
        functools.partial(local, mesh.shape["blk"], mesh.shape["win"]),
        mesh=mesh,
        in_specs=(P("win", None, "blk"), P("blk")),
        out_specs=P(None, "win", None, "blk", None),
        check_vma=False,
    )
```

time: 172 us -> 108 us (0.63)
  waiting for transfers between devices: 125 us -> 0 us
  Pallas kernels: 0 us -> 95.9 us
  matrix products: 16.2 us -> 0 us
  starting transfers between devices: 7.69 us -> 0 us
  local copies, waits for them, and re-layouts: 8.17 us -> 3.31 us
  blocking collectives: 3.79 us -> 0 us
    ppermute x4 -> x0, waiting for transfers between devices: 101 us -> none  [shifted(): return lax.ppermute(value, axis, pairs)]
    pallas_call x0 -> x1, Pallas kernels: none -> 95.9 us  [local(): pl.pallas_call(functools.partial(kernel, blocks, bands), out_shape=jax.Sh...]
    all_to_all x1 -> x0, waiting for transfers between devices: 24.3 us -> none  [regroup(): lax.all_to_all(spectra, 'win', split_axis=1, concat_axis=0, tiled=True)]
    dot_general x9 -> x0, matrix products: 16.2 us -> none  [the longest x1 6.06 us: local(): jnp.einsum('rt,wtc->wrc', transform, traces, preferred_element_type=jnp.f...]
    mul x5 -> x1, other arithmetic: 0.93 us -> 7.84 us  [local(): return (acc * norm_scale).reshape(ROUNDS, 1, 2, channels, channels)]
    convert_element_type x2 -> x0, local copies, waits for them, and re-layouts: 5.18 us -> none  [the longest x1 2.94 us: local(): spectra = jnp.einsum('rt,wtc->wrc', transform, traces, preferred_element_...]
    all_to_all x1 -> x0, starting transfers between devices: 4.93 us -> none  [regroup(): lax.all_to_all(spectra, 'win', split_axis=1, concat_axis=0, tiled=True)]
    broadcast_in_dim x1 -> x0, other arithmetic: 3.86 us -> none  [local(): return jnp.stack(results)[:, None]]
  transfers between devices with their start and end apart: 5 -> 0, of which waited for: 5 -> 0; matrix products, arithmetic and copies ran while one was open for 5% -> 0% of each run, Pallas kernels for 0% -> 0%
where the time goes in v1:
time: 108 us; the launch traced here: 107 us
  Pallas kernels  95.9 us (89%)
  other arithmetic  7.84 us (7%)
  local copies, waits for them, and re-layouts  3.31 us (3%)
    pallas_call x1, Pallas kernels, local(): pl.pallas_call(functools.partial(kernel, blocks, bands), out_shape=jax.Sh...  95.9 us
    mul x1, other arithmetic, local(): return (acc * norm_scale).reshape(ROUNDS, 1, 2, channels, channels)  7.84 us
    unnamed x6, local copies, waits for them, and re-layouts  3.31 us

profile of v1, /device:TPU:27, one launch (start us, length us, event | category | flops | bytes accessed | tf_op | source)
XLA Modules:
  0.0 107.0 jit_solution(2187863307295954612)
XLA Ops:
  0.0 0.0 copy-start
  0.0 1.6 %copy-done = bf16[4,512,512]{2,1,0:T(8,128)(2,1)S(1)} copy-done((bf16[4,512,512]{2,1,0:T(8,128)(2,1)S(1)}, bf16[4,512,512]{2,1,0:T(8,128)(2,1)}, u32[]{:S(2)}) %copy-start) | copy-done | bytes 2097176
  1.6 0.0 copy-start.1
  1.6 0.7 copy-done.1
  2.3 0.0 copy-start.2
  2.3 1.0 copy-done.2
  3.3 95.9 %shard_map.37 = f32[4,1024,512]{2,1,0:T(8,128)} custom-call(bf16[4,512,512]{2,1,0:T(8,128)(2,1)S(1)} %copy-done, bf16[2,256,512]{2,1,0:T(8,128)(2,1)S(1)} %copy-done.2, s32[1,512]{1,0:T(1,128)S(1)} %bitcast.4), custom_call_target="tpu_custom_call" | custom-call | flops 9663676416 | bytes 16777216 | tf_op jit(solution)/shard_map/pallas_call | solution.py:242
  99.2 7.8 %broadcast_multiply_fusion = f32[4,1024,512]{2,1,0:T(8,128)} fusion(f32[4,1024,512]{2,1,0:T(8,128)} %shard_map.37), kind=kLoop, calls=%fused_computation | loop fusion | flops 2097152 | bytes 16777216 | tf_op jit(solution)/shard_map/mul | solution.py:262
Async XLA Ops:
  0.0 1.6 %copy-start = (bf16[4,512,512]{2,1,0:T(8,128)(2,1)S(1)}, bf16[4,512,512]{2,1,0:T(8,128)(2,1)}, u32[]{:S(2)}) copy-start(bf16[4,512,512]{2,1,0:T(8,128)(2,1)} %traces.1) | copy-start | bytes 6291460
  1.6 0.7 copy-start.1
  2.3 1.0 copy-start.2

commit v2 on v1

v2 whole, which is shorter than its diff:
```python
import functools
import math

import jax
import jax.numpy as jnp
import ml_dtypes
import numpy as np
from jax import lax
from jax.experimental import pallas as pl
from jax.experimental.pallas import tpu as pltpu
from jax.sharding import PartitionSpec as P

ROUNDS = 4
CHUNK_BINS = 16
WATER_LEVEL = 0.5
MESH = pl.DeviceIdType.MESH


def dft_table(samples, bands, bins):
    width = samples // 2 // bands
    order = np.arange(samples // 2).reshape(bands, width // bins, 1, bins)
    order = np.broadcast_to(order, (bands, width // bins, 2, bins))
    time = np.arange(samples)
    phase = order[..., None] * time % samples
    angles = 2.0 * np.pi / samples * phase
    taper = 0.5 - 0.5 * np.cos(2.0 * np.pi / samples * time)
    imag = np.array([False, True])[None, None, :, None, None]
    entries = np.where(imag, -np.sin(angles), np.cos(angles)) * taper
    return entries.reshape(bands, 2 * width, samples).astype(np.float32).astype(ml_dtypes.bfloat16)


DEPTH = 3


def kernel(
    blocks, bands, traces, table, mask, out,
    buf, stage, acc, gathered, level,
    send_y, recv_y, send_z, send_x, send_sib, recv_blk,
    send_lw, recv_lw, send_lb, recv_lb, send_out,
):
    me = lax.axis_index("blk")
    band = lax.axis_index("win")
    core = lax.rem(me, 2)
    odd = lax.rem(me // 2, 2)
    pieces, local_windows, rows, channels = buf.shape[1:]
    chunks = pieces // bands
    windows = local_windows * bands
    bins = rows // 2
    bin_count = chunks * bins * bands
    relay_lag = DEPTH
    forward_lag = relay_lag + 2
    cross_lag = -(-forward_lag // bands)

    def at(step):
        return (lax.rem(me + step + blocks, blocks), band)

    def peer(step):
        return (me, lax.rem(band + step, bands))

    sibling = (me + 1 - 2 * core, band)
    others = [at(s) for s in range(-ROUNDS, ROUNDS + 1) if s] + [peer(d) for d in range(1, bands)]
    barrier = pltpu.get_barrier_semaphore()
    for other in others:
        pl.semaphore_signal(barrier, inc=1, device_id=other, device_id_type=MESH)

    def remote(src, dst, send, recv, target):
        return pltpu.make_async_remote_copy(
            src_ref=src, dst_ref=dst, send_sem=send, recv_sem=recv,
            device_id=target, device_id_type=MESH,
        )

    def copy_y(d, q):
        return remote(
            stage.at[d - 1, q], buf.at[0, q * bands + bands - d],
            send_y.at[d - 1, q], recv_y.at[d - 1, q], peer(d),
        )

    def copy_z(u):
        return remote(buf.at[0, u], buf.at[4, u], send_z.at[u], recv_blk.at[3, u], at(-4))

    def copy_x(slot, step, u):
        return remote(buf.at[slot, u], buf.at[2, u], send_x.at[u], recv_blk.at[1, u], at(step))

    def copy_sib(slot, pair, u):
        return remote(
            buf.at[slot, u], buf.at[1 + 2 * pair, u],
            send_sib.at[pair, u], recv_blk.at[2 * pair, u], sibling,
        )

    def copy_lw(d):
        return remote(
            gathered.at[0], gathered.at[bands - d], send_lw.at[d - 1], recv_lw.at[d - 1], peer(d)
        )

    def copy_lb(r):
        return remote(level.at[0], level.at[r], send_lb.at[r - 1], recv_lb.at[r - 1], at(-r))

    def copy_out(r):
        return pltpu.make_async_copy(acc.at[r], out.at[r], send_out.at[r])

    def spectrum(which, window):
        value = jnp.dot(table[which], traces[window], preferred_element_type=jnp.float32)
        value = value.astype(jnp.bfloat16)
        wide = value.astype(jnp.float32)
        gathered[0] += (wide * wide).reshape(-1, 8, channels).sum(axis=0)
        return value.reshape(chunks, rows, channels)

    def parts(slot, q):
        def get(w):
            piece = q * bands + w // local_windows
            value = buf[slot, piece, w % local_windows].astype(jnp.float32)
            return value[:bins], value[bins:]
        return get

    def factor(slot, spec):
        total = None
        for w in range(windows):
            re, im = spec(w)
            term = re * re + im * im
            total = term if total is None else total + term
        power = total * (1.0 / windows)
        mean = jnp.sum(level[slot, 0], axis=0, keepdims=True) * (1.0 / (windows * bin_count))
        return level[slot, 1][:1] * lax.rsqrt(power + WATER_LEVEL * mean + 1e-06)

    def cross(q):
        spec = parts(0, q)
        scale = factor(0, spec)
        lhs = []
        for w in range(windows):
            re, im = spec(w)
            re, im = re * scale, im * scale
            lhs.append(jnp.concatenate([
                jnp.concatenate([re, -im], axis=1), jnp.concatenate([im, re], axis=1)
            ], axis=0).astype(jnp.bfloat16))
        lhs = jnp.concatenate(lhs, axis=0).T
        for slot in (2, 4, 1, 3):
            if slot in (1, 3):
                for h in range(bands):
                    copy_sib(0, slot // 2, q * bands + h).wait_recv()
            spec = parts(slot, q)
            scale = factor(slot, spec)
            rhs = []
            for w in range(windows):
                re, im = spec(w)
                rhs.append(jnp.concatenate([re * scale, im * scale], axis=0).astype(jnp.bfloat16))
            acc[slot - 1] += jnp.dot(
                lhs, jnp.concatenate(rhs, axis=0), preferred_element_type=jnp.float32
            )

            @pl.when(q == chunks - 1)
            def _():
                copy_out(slot - 1).start()

    gathered[0] = jnp.zeros(gathered.shape[1:], jnp.float32)
    for d in range(1, bands):
        which = lax.rem(band + d, bands)
        for w in range(local_windows):
            stage[d - 1, :, w] = spectrum(which, w)
    pl.semaphore_wait(barrier, len(others))
    for q in range(min(2, chunks)):
        for d in range(bands - 1, 0, -1):
            copy_y(d, q).start()
    for w in range(local_windows):
        value = spectrum(band, w)
        for q in range(chunks):
            buf[0, q * bands, w] = value[q]
    level[0, 1] = jnp.broadcast_to(mask[...].astype(jnp.float32), (8, channels))

    def send_own(t, h):
        u = t * bands + h
        if h:
            copy_y(bands - h, t).wait_recv()

        @pl.when(u >= DEPTH)
        def _():
            copy_z(u - DEPTH).wait_send()

        copy_z(u).start()

        @pl.when(odd == 1)
        def _():
            copy_x(0, -2, u).start()

        @pl.when(core == 1)
        def _():
            copy_sib(0, 0, u).start()

    def relay(u):
        copy_z(u).wait_recv()

        @pl.when(odd == 0)
        def _():
            copy_x(4, 2, u).start()

        @pl.when(core == 0)
        def _():
            copy_sib(4, 1, u).start()

    def forward(u):
        copy_x(0, -2, u).wait_recv()
        copy_sib(2, core, u).start()

    def step(t, _):
        for h in range(bands):
            u = t * bands + h

            @pl.when(t < chunks)
            def _():
                send_own(t, h)

            if h == bands - 1:
                @pl.when(t + 2 < chunks)
                def _():
                    for d in range(bands - 1, 0, -1):
                        copy_y(d, t + 2).start()

            @pl.when((u >= relay_lag) & (u < pieces + relay_lag))
            def _():
                relay(u - relay_lag)

            @pl.when((u >= forward_lag) & (u < pieces + forward_lag))
            def _():
                forward(u - forward_lag)

        @pl.when(t == 0)
        def _():
            for d in range(1, bands):
                copy_lw(d).start()
            for slot in range(ROUNDS):
                acc[slot] = jnp.zeros(acc.shape[1:], jnp.float32)
            for d in range(1, bands):
                copy_lw(d).wait()
            level[0, 0] = jnp.sum(gathered[...], axis=0)
            for r in range(1, ROUNDS + 1):
                copy_lb(r).start()

        @pl.when(t == cross_lag)
        def _():
            for r in range(1, ROUNDS + 1):
                copy_lb(r).wait()

        @pl.when(t >= cross_lag)
        def _():
            cross(t - cross_lag)
        return 0

    lax.fori_loop(0, chunks + cross_lag, step, 0)

    for q in range(chunks):
        for d in range(1, bands):
            copy_y(d, q).wait_send()
    for u in range(pieces):
        if u >= pieces - DEPTH:
            copy_z(u).wait_send()
        copy_x(0, -2, u).wait_send()
        copy_sib(0, 0, u).wait_send()
        copy_sib(0, 1, u).wait_send()
    for r in range(ROUNDS):
        copy_out(r).wait()


def local(blocks, bands, traces, channel_mask):
    local_windows, samples, channels = traces.shape
    windows = local_windows * bands
    width = samples // 2 // bands
    bins = min(CHUNK_BINS, width)
    chunks = width // bins
    pieces = chunks * bands
    table = jnp.asarray(dft_table(samples, bands, bins))
    vmem = pl.BlockSpec(memory_space=pltpu.VMEM)
    dma = pltpu.SemaphoreType.DMA
    flops = 2 * samples * samples * channels * local_windows
    flops += 2 * ROUNDS * 2 * channels * channels * windows * 2 * width
    acc = pl.pallas_call(
        functools.partial(kernel, blocks, bands),
        out_shape=jax.ShapeDtypeStruct((ROUNDS, 2 * channels, channels), jnp.float32),
        in_specs=[vmem] * 3,
        out_specs=pl.BlockSpec(memory_space=pl.ANY),
        scratch_shapes=[
            pltpu.VMEM((ROUNDS + 1, pieces, local_windows, 2 * bins, channels), jnp.bfloat16),
            pltpu.VMEM((bands - 1, chunks, local_windows, 2 * bins, channels), jnp.bfloat16),
            pltpu.VMEM((ROUNDS, 2 * channels, channels), jnp.float32),
            pltpu.VMEM((bands, 8, channels), jnp.float32),
            pltpu.VMEM((ROUNDS + 1, 2, 8, channels), jnp.float32),
            dma((bands - 1, chunks)), dma((bands - 1, chunks)),
            dma((pieces,)), dma((pieces,)), dma((2, pieces)), dma((ROUNDS, pieces)),
            dma((bands - 1,)), dma((bands - 1,)), dma((ROUNDS,)), dma((ROUNDS,)), dma((ROUNDS,)),
        ],
        compiler_params=pltpu.CompilerParams(
            collective_id=0, has_side_effects=True, vmem_limit_bytes=32 * 2**20
        ),
        cost_estimate=pl.CostEstimate(flops=flops, bytes_accessed=2**24, transcendentals=0),
    )(traces, table, channel_mask[None])
    norm_scale = 1.0 / math.sqrt(windows * width)
    return (acc * norm_scale).reshape(ROUNDS, 1, 2, channels, channels)


def solution(mesh):
    return jax.shard_map(
        functools.partial(local, mesh.shape["blk"], mesh.shape["win"]),
        mesh=mesh,
        in_specs=(P("win", None, "blk"), P("blk")),
        out_specs=P(None, "win", None, "blk", None),
        check_vma=False,
    )
```

time: 108 us -> 75.7 us (0.70)
  Pallas kernels: 95.9 us -> 67.7 us
  other arithmetic: 7.84 us -> 4.45 us
    pallas_call x1, Pallas kernels: 95.9 us -> 67.7 us  [local(): pl.pallas_call(functools.partial(kernel, blocks, bands), out_shape=jax.Sh...]
    mul x1, other arithmetic: 7.84 us -> 4.45 us  [local(): return (acc * norm_scale).reshape(ROUNDS, 1, 2, channels, channels)]
where the time goes in v2:
time: 75.7 us; the launch traced here: 75.5 us
  Pallas kernels  67.7 us (89%)
  other arithmetic  4.45 us (6%)
  local copies, waits for them, and re-layouts  3.31 us (4%)
    pallas_call x1, Pallas kernels, local(): pl.pallas_call(functools.partial(kernel, blocks, bands), out_shape=jax.Sh...  67.7 us
    mul x1, other arithmetic, local(): return (acc * norm_scale).reshape(ROUNDS, 1, 2, channels, channels)  4.45 us
    unnamed x6, local copies, waits for them, and re-layouts  3.31 us

profile of v2, /device:TPU:27, one launch (start us, length us, event | category | flops | bytes accessed | tf_op | source)
XLA Modules:
  0.0 75.5 jit_solution(14450895572568488535)
XLA Ops:
  0.0 0.0 copy-start
  0.0 1.6 %copy-done = bf16[4,512,512]{2,1,0:T(8,128)(2,1)S(1)} copy-done((bf16[4,512,512]{2,1,0:T(8,128)(2,1)S(1)}, bf16[4,512,512]{2,1,0:T(8,128)(2,1)}, u32[]{:S(2)}) %copy-start) | copy-done | bytes 2097176
  1.6 0.0 copy-start.1
  1.6 0.7 copy-done.1
  2.3 0.0 copy-start.2
  2.3 1.0 %copy-done.2 = bf16[2,256,512]{2,1,0:T(8,128)(2,1)S(1)} copy-done((bf16[2,256,512]{2,1,0:T(8,128)(2,1)S(1)}, bf16[2,256,512]{2,1,0:T(8,128)(2,1)}, u32[]{:S(2)}) %copy-start.2) | copy-done | bytes 524312
  3.3 67.7 %shard_map.37 = f32[4,1024,512]{2,1,0:T(8,128)S(1)} custom-call(bf16[4,512,512]{2,1,0:T(8,128)(2,1)S(1)} %copy-done, bf16[2,256,512]{2,1,0:T(8,128)(2,1)S(1)} %copy-done.2, s32[1,512]{1,0:T(1,128)S(1)} %bitcast.4), custom_call_target="tpu_custom_call" | custom-call | flops 9663676416 | bytes 16777216 | tf_op jit(solution)/shard_map/pallas_call | solution.py:274
  71.1 4.4 %broadcast_multiply_fusion = f32[4,1024,512]{2,1,0:T(8,128)} fusion(f32[4,1024,512]{2,1,0:T(8,128)S(1)} %shard_map.37), kind=kLoop, calls=%fused_computation | loop fusion | flops 2097152 | bytes 16777216 | tf_op jit(solution)/shard_map/mul | solution.py:295
Async XLA Ops:
  0.0 1.6 %copy-start = (bf16[4,512,512]{2,1,0:T(8,128)(2,1)S(1)}, bf16[4,512,512]{2,1,0:T(8,128)(2,1)}, u32[]{:S(2)}) copy-start(bf16[4,512,512]{2,1,0:T(8,128)(2,1)} %traces.1) | copy-start | bytes 6291460
  1.6 0.7 copy-start.1
  2.3 1.0 %copy-start.2 = (bf16[2,256,512]{2,1,0:T(8,128)(2,1)S(1)}, bf16[2,256,512]{2,1,0:T(8,128)(2,1)}, u32[]{:S(2)}) copy-start(bf16[2,256,512]{2,1,0:T(8,128)(2,1)} %constant.4.clone.table) | copy-start | bytes 1572868

commit v3 on v2

--- a/solution.py
+++ b/solution.py
@@ -11,7 +11,7 @@
 from jax.sharding import PartitionSpec as P
 
 ROUNDS = 4
-CHUNK_BINS = 16
+CHUNK_BINS = 8
 WATER_LEVEL = 0.5
 MESH = pl.DeviceIdType.MESH
 
@@ -29,14 +29,14 @@
     return entries.reshape(bands, 2 * width, samples).astype(np.float32).astype(ml_dtypes.bfloat16)
 
 
-DEPTH = 3
+DEPTH = 4
 
 
 def kernel(
-    blocks, bands, traces, table, mask, out,
-    buf, stage, acc, gathered, level,
+    blocks, bands, traces, table, mask, acc,
+    buf, stage, gathered, level,
     send_y, recv_y, send_z, send_x, send_sib, recv_blk,
-    send_lw, recv_lw, send_lb, recv_lb, send_out,
+    send_lw, recv_lw, send_lb, recv_lb,
 ):
     me = lax.axis_index("blk")
     band = lax.axis_index("win")
@@ -94,9 +94,6 @@
 
     def copy_lb(r):
         return remote(level.at[0], level.at[r], send_lb.at[r - 1], recv_lb.at[r - 1], at(-r))
-
-    def copy_out(r):
-        return pltpu.make_async_copy(acc.at[r], out.at[r], send_out.at[r])
 
     def spectrum(which, window):
         value = jnp.dot(table[which], traces[window], preferred_element_type=jnp.float32)
@@ -147,10 +144,6 @@
                 lhs, jnp.concatenate(rhs, axis=0), preferred_element_type=jnp.float32
             )
 
-            @pl.when(q == chunks - 1)
-            def _():
-                copy_out(slot - 1).start()
-
     gathered[0] = jnp.zeros(gathered.shape[1:], jnp.float32)
     for d in range(1, bands):
         which = lax.rem(band + d, bands)
@@ -255,8 +248,6 @@
         copy_x(0, -2, u).wait_send()
         copy_sib(0, 0, u).wait_send()
         copy_sib(0, 1, u).wait_send()
-    for r in range(ROUNDS):
-        copy_out(r).wait()
 
 
 def local(blocks, bands, traces, channel_mask):
@@ -275,16 +266,15 @@
         functools.partial(kernel, blocks, bands),
         out_shape=jax.ShapeDtypeStruct((ROUNDS, 2 * channels, channels), jnp.float32),
         in_specs=[vmem] * 3,
-        out_specs=pl.BlockSpec(memory_space=pl.ANY),
+        out_specs=vmem,
         scratch_shapes=[
             pltpu.VMEM((ROUNDS + 1, pieces, local_windows, 2 * bins, channels), jnp.bfloat16),
             pltpu.VMEM((bands - 1, chunks, local_windows, 2 * bins, channels), jnp.bfloat16),
-            pltpu.VMEM((ROUNDS, 2 * channels, channels), jnp.float32),
             pltpu.VMEM((bands, 8, channels), jnp.float32),
             pltpu.VMEM((ROUNDS + 1, 2, 8, channels), jnp.float32),
             dma((bands - 1, chunks)), dma((bands - 1, chunks)),
             dma((pieces,)), dma((pieces,)), dma((2, pieces)), dma((ROUNDS, pieces)),
-            dma((bands - 1,)), dma((bands - 1,)), dma((ROUNDS,)), dma((ROUNDS,)), dma((ROUNDS,)),
+            dma((bands - 1,)), dma((bands - 1,)), dma((ROUNDS,)), dma((ROUNDS,)),
         ],
         compiler_params=pltpu.CompilerParams(
             collective_id=0, has_side_effects=True, vmem_limit_bytes=32 * 2**20

time: 75.7 us -> 75.5 us (level)
  no operation moved by 1% of the time
where the time goes in v3:
time: 75.5 us; the launch traced here: 75.3 us
  Pallas kernels  67.5 us (89%)
  other arithmetic  4.45 us (6%)
  local copies, waits for them, and re-layouts  3.31 us (4%)
    pallas_call x1, Pallas kernels, local(): pl.pallas_call(functools.partial(kernel, blocks, bands), out_shape=jax.Sh...  67.5 us
    mul x1, other arithmetic, local(): return (acc * norm_scale).reshape(ROUNDS, 1, 2, channels, channels)  4.45 us
    unnamed x6, local copies, waits for them, and re-layouts  3.31 us

profile of v3, /device:TPU:27, one launch (start us, length us, event | category | flops | bytes accessed | tf_op | source)
XLA Modules:
  0.0 75.3 jit_solution(10859428511021883478)
XLA Ops:
  0.0 0.0 copy-start
  0.0 1.6 %copy-done = bf16[4,512,512]{2,1,0:T(8,128)(2,1)S(1)} copy-done((bf16[4,512,512]{2,1,0:T(8,128)(2,1)S(1)}, bf16[4,512,512]{2,1,0:T(8,128)(2,1)}, u32[]{:S(2)}) %copy-start) | copy-done | bytes 2097176
  1.6 0.0 copy-start.1
  1.6 0.7 copy-done.1
  2.3 0.0 copy-start.2
  2.3 1.0 %copy-done.2 = bf16[2,256,512]{2,1,0:T(8,128)(2,1)S(1)} copy-done((bf16[2,256,512]{2,1,0:T(8,128)(2,1)S(1)}, bf16[2,256,512]{2,1,0:T(8,128)(2,1)}, u32[]{:S(2)}) %copy-start.2) | copy-done | bytes 524312
  3.3 67.5 %shard_map.37 = f32[4,1024,512]{2,1,0:T(8,128)S(1)} custom-call(bf16[4,512,512]{2,1,0:T(8,128)(2,1)S(1)} %copy-done, bf16[2,256,512]{2,1,0:T(8,128)(2,1)S(1)} %copy-done.2, s32[1,512]{1,0:T(1,128)S(1)} %bitcast.4), custom_call_target="tpu_custom_call" | custom-call | flops 9663676416 | bytes 16777216 | tf_op jit(solution)/shard_map/pallas_call | solution.py:265
  70.9 4.4 %broadcast_multiply_fusion = f32[4,1024,512]{2,1,0:T(8,128)} fusion(f32[4,1024,512]{2,1,0:T(8,128)S(1)} %shard_map.37), kind=kLoop, calls=%fused_computation | loop fusion | flops 2097152 | bytes 16777216 | tf_op jit(solution)/shard_map/mul | solution.py:285
Async XLA Ops:
  0.0 1.6 %copy-start = (bf16[4,512,512]{2,1,0:T(8,128)(2,1)S(1)}, bf16[4,512,512]{2,1,0:T(8,128)(2,1)}, u32[]{:S(2)}) copy-start(bf16[4,512,512]{2,1,0:T(8,128)(2,1)} %traces.1) | copy-start | bytes 6291460
  1.6 0.7 copy-start.1
  2.3 1.0 %copy-start.2 = (bf16[2,256,512]{2,1,0:T(8,128)(2,1)S(1)}, bf16[2,256,512]{2,1,0:T(8,128)(2,1)}, u32[]{:S(2)}) copy-start(bf16[2,256,512]{2,1,0:T(8,128)(2,1)} %constant.4.clone.table) | copy-start | bytes 1572868

commit v4 on v3

--- a/solution.py
+++ b/solution.py
@@ -221,6 +221,9 @@
                 copy_lw(d).start()
             for slot in range(ROUNDS):
                 acc[slot] = jnp.zeros(acc.shape[1:], jnp.float32)
+
+        @pl.when(t == 1)
+        def _():
             for d in range(1, bands):
                 copy_lw(d).wait()
             level[0, 0] = jnp.sum(gathered[...], axis=0)

time: 75.5 us -> 73.8 us (0.977)
  Pallas kernels: 67.5 us -> 65.8 us
    pallas_call x1, Pallas kernels: 67.5 us -> 65.8 us  [local(): pl.pallas_call(functools.partial(kernel, blocks, bands), out_shape=jax.Sh...]
where the time goes in v4:
time: 73.8 us; the launch traced here: 73.6 us
  Pallas kernels  65.8 us (89%)
  other arithmetic  4.45 us (6%)
  local copies, waits for them, and re-layouts  3.31 us (4%)
    pallas_call x1, Pallas kernels, local(): pl.pallas_call(functools.partial(kernel, blocks, bands), out_shape=jax.Sh...  65.8 us
    mul x1, other arithmetic, local(): return (acc * norm_scale).reshape(ROUNDS, 1, 2, channels, channels)  4.45 us
    unnamed x6, local copies, waits for them, and re-layouts  3.31 us

profile of v4, /device:TPU:27, one launch (start us, length us, event | category | flops | bytes accessed | tf_op | source)
XLA Modules:
  0.0 73.6 jit_solution(1907303230346432803)
XLA Ops:
  0.0 0.0 copy-start
  0.0 1.6 %copy-done = bf16[4,512,512]{2,1,0:T(8,128)(2,1)S(1)} copy-done((bf16[4,512,512]{2,1,0:T(8,128)(2,1)S(1)}, bf16[4,512,512]{2,1,0:T(8,128)(2,1)}, u32[]{:S(2)}) %copy-start) | copy-done | bytes 2097176
  1.6 0.0 copy-start.1
  1.6 0.7 copy-done.1
  2.3 0.0 copy-start.2
  2.3 1.0 %copy-done.2 = bf16[2,256,512]{2,1,0:T(8,128)(2,1)S(1)} copy-done((bf16[2,256,512]{2,1,0:T(8,128)(2,1)S(1)}, bf16[2,256,512]{2,1,0:T(8,128)(2,1)}, u32[]{:S(2)}) %copy-start.2) | copy-done | bytes 524312
  3.3 65.8 %shard_map.37 = f32[4,1024,512]{2,1,0:T(8,128)S(1)} custom-call(bf16[4,512,512]{2,1,0:T(8,128)(2,1)S(1)} %copy-done, bf16[2,256,512]{2,1,0:T(8,128)(2,1)S(1)} %copy-done.2, s32[1,512]{1,0:T(1,128)S(1)} %bitcast.4), custom_call_target="tpu_custom_call" | custom-call | flops 9663676416 | bytes 16777216 | tf_op jit(solution)/shard_map/pallas_call | solution.py:268
  69.2 4.4 %broadcast_multiply_fusion = f32[4,1024,512]{2,1,0:T(8,128)} fusion(f32[4,1024,512]{2,1,0:T(8,128)S(1)} %shard_map.37), kind=kLoop, calls=%fused_computation | loop fusion | flops 2097152 | bytes 16777216 | tf_op jit(solution)/shard_map/mul | solution.py:288
Async XLA Ops:
  0.0 1.6 %copy-start = (bf16[4,512,512]{2,1,0:T(8,128)(2,1)S(1)}, bf16[4,512,512]{2,1,0:T(8,128)(2,1)}, u32[]{:S(2)}) copy-start(bf16[4,512,512]{2,1,0:T(8,128)(2,1)} %traces.1) | copy-start | bytes 6291460
  1.6 0.7 copy-start.1
  2.3 1.0 %copy-start.2 = (bf16[2,256,512]{2,1,0:T(8,128)(2,1)S(1)}, bf16[2,256,512]{2,1,0:T(8,128)(2,1)}, u32[]{:S(2)}) copy-start(bf16[2,256,512]{2,1,0:T(8,128)(2,1)} %constant.4.clone.table) | copy-start | bytes 1572868
